TPU v7x, 32 devices: a whole 2x2x4 slice. The times are simulated.
32 devices in a mesh: ctx: 8 (over y, x, core), head: 4 (over z).
Axes of the slice: x: 2, y: 2, z: 4, core: 2. Of those that a mesh axis runs over, the one named last changes fastest.
Arguments:
- mixer_in: bfloat16 [1536, 16384], P('ctx', 'head'), may hold values from -6 to 6
- step_raw: float32 [1536, 256], P('ctx', 'head'), may hold values from -13.5 to -1
- decay_log: float32 [256], P('head'), may hold values from -0.5 to 1
- b_proj: bfloat16 [1536, 1024], P('ctx', 'head'), may hold values from -6 to 6
- c_proj: bfloat16 [1536, 1024], P('ctx', 'head'), may hold values from -6 to 6
- mixer_grad: bfloat16 [1536, 16384], P('ctx', 'head'), may hold values from -6 to 6
- queries: bfloat16 [1536, 4096], P(('ctx', 'head')), may hold values from -200 to 200
- keys_in: bfloat16 [1536, 1024], P(('ctx', 'head')), may hold values from -6 to 6
- values: bfloat16 [1536, 1024], P(('ctx', 'head')), may hold values from -6 to 6
- out_grad: bfloat16 [1536, 4096], P(('ctx', 'head')), may hold values from -6 to 6
Outputs:
- grad_input: bfloat16 [1536, 16384], P('ctx', 'head')
- grad_step: float32 [1536, 256], P('ctx', 'head')
- grad_bproj: float32 [1536, 1024], P('ctx', 'head')
- grad_cproj: float32 [1536, 1024], P('ctx', 'head')
- grad_query: bfloat16 [1536, 4096], P(('ctx', 'head'))
- grad_key: bfloat16 [1536, 1024], P(('ctx', 'head'))
- grad_value: bfloat16 [1536, 1024], P(('ctx', 'head'))
All inputs are finite; a program needn't handle non-finite values.
Results may differ from a plain program's by a relative error of at most 0.012.
Values may be sent and summed in bfloat16 or wider, within the bound.
A program may use at most 128 MiB of HBM per device.

v0:
```python
import functools

import jax
import jax.numpy as jnp
from jax import lax
from jax.experimental import pallas as pl
from jax.experimental.pallas import tpu as pltpu
from jax.sharding import PartitionSpec as P

STATE = 128
QHEADS = 32
KV_HEADS = 8
HEAD_DIM = 128
SUB = 64
GROUP = QHEADS // KV_HEADS
F32 = jnp.float32
BF = jnp.bfloat16


def mm(a, b, ca=1, cb=0, precision=None):
    return lax.dot_general(
        a, b, (((ca,), (cb,)), ((), ())), preferred_element_type=F32, precision=precision
    )


def split(v):
    hi = v.astype(BF)
    return hi, (v - hi.astype(F32)).astype(BF)


def body(
    nc, nh, tile,
    x_ref, step_ref, decay_ref, b_ref, c_ref, dy_ref, q_ref, k_ref, v_ref, o_ref,
    gx_ref, gs_ref, gb_ref, gc_ref, gq_ref, gk_ref, gv_ref,
    qbuf, obuf, kbuf, vbuf, kv, dkv, dkvin, kvb, q4, o4, dqb,
    s_scr, dp_scr,
    sloc, srecv, sin, decloc, decrecv,
    vec_hi, vec_lo, xt_scr, dyg_scr, gm, gmt, dg, acc, dbc,
    h_send, h_recv, kv_send, kv_recv, st_send, st_recv, dc_send, dc_recv,
    bk_send, bk_recv, dkv_send, dkv_recv, back_send, back_recv,
):
    L, CH = x_ref.shape
    H = step_ref.shape[1]
    width = CH // H
    groups = b_ref.shape[1] // STATE
    rows = q_ref.shape[0]
    qc = q_ref.shape[1] // nh
    kc = k_ref.shape[1] // nh
    nkv = kc // HEAD_DIM
    chunk = CH // nc
    per = tile // chunk
    tpg = CH // groups // tile
    nsub = L // SUB
    me = lax.axis_index("ctx")
    mh = lax.axis_index("head")
    factor = HEAD_DIM ** (-0.5)

    barrier = pltpu.get_barrier_semaphore()
    for d in range(1, nc):
        pl.semaphore_signal(barrier, inc=1, device_id={"ctx": lax.rem(me + d, nc)},
                            device_id_type=pl.DeviceIdType.MESH)
    for d in range(1, nh):
        pl.semaphore_signal(barrier, inc=1, device_id={"head": lax.rem(mh + d, nh)},
                            device_id_type=pl.DeviceIdType.MESH)
    pl.semaphore_wait(barrier, nc - 1 + nh - 1)

    def remote(src, dst, ss, rs, axis, peer):
        return pltpu.make_async_remote_copy(
            src_ref=src, dst_ref=dst, send_sem=ss, recv_sem=rs,
            device_id={axis: peer}, device_id_type=pl.DeviceIdType.MESH)

    def cols(ref, at, n):
        return ref.at[:, pl.ds(pl.multiple_of(at * n, 128), n)]

    head_copies = []
    for n, (ref, buf, w) in enumerate(
        ((k_ref, kbuf, kc), (v_ref, vbuf, kc), (q_ref, qbuf, qc), (o_ref, obuf, qc))):
        for d in range(1, nh):
            peer = lax.rem(mh + d, nh)
            cp = remote(cols(ref, peer, w), buf.at[mh], h_send.at[n, d], h_recv.at[n, d], "head", peer)
            cp.start()
            head_copies.append(cp)
    for ref, buf, w in ((k_ref, kbuf, kc), (v_ref, vbuf, kc), (q_ref, qbuf, qc), (o_ref, obuf, qc)):
        buf[mh] = ref[:, pl.ds(pl.multiple_of(mh * w, 128), w)]

    high = lax.Precision.HIGHEST
    raw = step_ref[...]
    e = jnp.exp(raw)
    dt = jnp.log1p(e)
    rate = jnp.exp(decay_ref[...])
    ri = lax.broadcasted_iota(jnp.int32, (L, L), 0)
    ci = lax.broadcasted_iota(jnp.int32, (L, L), 1)
    tril = (ri >= ci).astype(F32)
    cum = mm(tril, -rate * dt, precision=high)
    last = cum[L - 1:L]
    refs = [jnp.zeros((1, H), F32)] + [cum[SUB * i - 1:SUB * i] for i in range(1, nsub)]
    a = jnp.concatenate([jnp.exp(cum[SUB * i:SUB * (i + 1)] - refs[i]) for i in range(nsub)], 0)
    vecs = [dt, a, jnp.exp(cum), jnp.exp(last - cum)]
    for i in range(nsub):
        vecs.append(jnp.exp(refs[i] - cum[:SUB * (i + 1)]))
    vecs.append(jnp.broadcast_to(jnp.exp(last), (16, H)))
    offs = []
    at = 0
    for v in vecs:
        hi, lo = split(v)
        offs.append((at, v.shape[0]))
        vec_hi[at:at + v.shape[0]] = hi
        vec_lo[at:at + v.shape[0]] = lo
        at += v.shape[0]

    def spread_of(t):
        hr = lax.broadcasted_iota(jnp.int32, (H, tile), 0)
        hc = lax.broadcasted_iota(jnp.int32, (H, tile), 1)
        one = (hc // width + t * (tile // width) == hr).astype(F32).astype(BF)

        def get(n):
            o, r = offs[n]
            return mm(vec_hi[o:o + r], one) + mm(vec_lo[o:o + r], one)
        return get

    def gather_of(t):
        hr = lax.broadcasted_iota(jnp.int32, (tile, H), 0)
        hc = lax.broadcasted_iota(jnp.int32, (tile, H), 1)
        one = (hr // width + t * (tile // width) == hc).astype(F32).astype(BF)

        def put(v):
            hi, lo = split(v)
            return mm(hi, one) + mm(lo, one)
        return put

    DT, AA, GROW, TAIL, B0 = 0, 1, 2, 3, 4
    DEC = B0 + nsub

    for g in range(groups):
        bg = b_ref[:, g * STATE:(g + 1) * STATE]
        cg = c_ref[:, g * STATE:(g + 1) * STATE]

        def summary(k, carry):
            t = g * tpg + k
            here = pl.ds(pl.multiple_of(t * tile, 128), tile)
            get = spread_of(t)
            xt = (x_ref[:, here].astype(F32) * get(DT) * get(TAIL)).astype(BF)
            dyg = (dy_ref[:, here].astype(F32) * get(GROW)).astype(BF)
            xt_scr[:, here] = xt
            dyg_scr[:, here] = dyg
            st = mm(bg, xt, 0, 0).astype(BF)
            pu = mm(cg, dyg, 0, 0).astype(BF)
            de = get(DEC)[:8]
            for m in range(per):
                part = slice(m * chunk, (m + 1) * chunk)
                sloc[t * per + m, 0] = st[:, part]
                sloc[t * per + m, 1] = pu[:, part]
                decloc[t * per + m] = de[:, part]
            return carry

        lax.fori_loop(0, tpg, summary, 0)

    st_copies = []
    for d in range(1, nc):
        peer = lax.rem(me + d, nc)
        for cp in (
            remote(decloc.at[peer], decrecv.at[me], dc_send.at[d], dc_recv.at[d], "ctx", peer),
            remote(sloc.at[peer], srecv.at[me], st_send.at[d], st_recv.at[d], "ctx", peer)):
            cp.start()
            st_copies.append(cp)
    srecv[me] = sloc[me]
    decrecv[me] = decloc[me]

    for cp in head_copies[:2 * (nh - 1)]:
        cp.wait_recv()
    for h in range(nh):
        kv[me, h, :, :kc] = kbuf[h]
        kv[me, h, :, kc:] = vbuf[h]

    def kv_copy(d):
        return remote(kv.at[me], kv.at[me], kv_send.at[d], kv_recv.at[d], "ctx", lax.rem(me + d, nc))

    for d in range(1, nc):
        @pl.when(me + d < nc)
        def _():
            kv_copy(d).start()

    for cp in head_copies[2 * (nh - 1):]:
        cp.wait_recv()
    for src, dst in ((qbuf, q4), (obuf, o4)):
        for k in range(nkv):
            for i in range(GROUP):
                for h in range(nh):
                    c0 = (k * GROUP + i) * HEAD_DIM
                    dst[k, i * L + h * rows:i * L + (h + 1) * rows] = src[h, :, c0:c0 + HEAD_DIM]

    for cp in st_copies:
        cp.wait()

    def prefix(n, run):
        sloc[n, 0] = run.astype(BF)
        return decrecv[n][:1] * run + srecv[n, 0].astype(F32)

    def suffix(n, run):
        n = nc - 1 - n
        sloc[n, 1] = run.astype(BF)
        return decrecv[n][:1] * run + srecv[n, 1].astype(F32)

    lax.fori_loop(0, nc, prefix, jnp.zeros((STATE, chunk), F32))
    lax.fori_loop(0, nc, suffix, jnp.zeros((STATE, chunk), F32))
    bk_copies = []
    for d in range(1, nc):
        peer = lax.rem(me + d, nc)
        cp = remote(sloc.at[peer], sin.at[me], bk_send.at[d], bk_recv.at[d], "ctx", peer)
        cp.start()
        bk_copies.append(cp)
    sin[me] = sloc[me]

    for d in range(1, nc):
        @pl.when(me - d >= 0)
        def _():
            kv_copy(d).wait_recv()

    Q = GROUP * L
    key_row = lax.broadcasted_iota(jnp.int32, (L, L), 0)
    qry = lax.broadcasted_iota(jnp.int32, (L, L), 1)
    diag = jnp.where(qry >= key_row, 0.0, -jnp.inf).astype(F32)
    diag4 = jnp.concatenate([diag] * GROUP, 1)

    for k in range(nkv):
        kcol = slice(k * HEAD_DIM, (k + 1) * HEAD_DIM)
        vcol = slice(kc + k * HEAD_DIM, kc + (k + 1) * HEAD_DIM)

        def kblock(j):
            return kv[j, :, :, kcol].reshape(L, HEAD_DIM)

        def score(j, m):
            s = mm(kblock(j), q4[k], 1, 1) * factor
            s = s + jnp.where(j == me, diag4, 0.0)
            s_scr[j] = s
            dp_scr[j] = mm(kv[j, :, :, vcol].reshape(L, HEAD_DIM), o4[k], 1, 1)
            return jnp.maximum(m, jnp.max(s, 0, keepdims=True))

        top = lax.fori_loop(0, me + 1, score, jnp.full((1, Q), -jnp.inf, F32))

        def total(j, c):
            p = jnp.exp(s_scr[j] - top)
            s_scr[j] = p
            return (c[0] + jnp.sum(p, 0, keepdims=True),
                    c[1] + jnp.sum(p * dp_scr[j], 0, keepdims=True))

        z = jnp.zeros((1, Q), F32)
        norm, dot = lax.fori_loop(0, me + 1, total, (z, z))
        inv = 1.0 / norm
        dot = dot * inv

        def grads(j, dqt):
            p = s_scr[j] * inv
            ds = (p * (dp_scr[j] - dot)).astype(BF)
            dkv[j, :, kcol] = (factor * mm(ds, q4[k])).astype(BF)
            dkv[j, :, vcol] = mm(p.astype(BF), o4[k]).astype(BF)
            return dqt + mm(kblock(j), ds, 0, 0)

        dqt = lax.fori_loop(0, me + 1, grads, jnp.zeros((HEAD_DIM, Q), F32))
        dq = (factor * dqt).T.astype(BF)
        for i in range(GROUP):
            for h in range(nh):
                c0 = (k * GROUP + i) * HEAD_DIM
                dqb[h, :, c0:c0 + HEAD_DIM] = dq[i * L + h * rows:i * L + (h + 1) * rows]

    def dkv_copy(d):
        peer = lax.rem(me - d + nc, nc)
        return remote(dkv.at[peer], dkvin.at[d], dkv_send.at[d], dkv_recv.at[d], "ctx", peer)

    for d in range(1, nc):
        @pl.when(me - d >= 0)
        def _():
            dkv_copy(d).start()
    back = []
    for d in range(1, nh):
        peer = lax.rem(mh + d, nh)
        cp = remote(dqb.at[peer], cols(gq_ref, mh, qc), back_send.at[0, d], back_recv.at[0, d], "head", peer)
        cp.start()
        back.append(cp)
    gq_ref[:, pl.ds(pl.multiple_of(mh * qc, 128), qc)] = dqb[mh]

    causal = ri >= ci
    for g in range(groups):
        bg = b_ref[:, g * STATE:(g + 1) * STATE]
        cg = c_ref[:, g * STATE:(g + 1) * STATE]
        gm[g] = jnp.where(causal, mm(cg, bg, 1, 1), 0.0).astype(BF)
        full = jnp.where(ri <= ci, mm(bg, cg, 1, 1), 0.0).astype(BF)
        for i in range(nsub):
            gmt[g, i] = full[:, i * SUB:(i + 1) * SUB]
    dg[...] = jnp.zeros_like(dg)
    acc[...] = jnp.zeros_like(acc)
    dbc[...] = jnp.zeros_like(dbc)
    for cp in bk_copies:
        cp.wait_recv()

    is_last = lax.broadcasted_iota(jnp.int32, (L, tile), 0) == L - 1
    for g in range(groups):
        bg = b_ref[:, g * STATE:(g + 1) * STATE]
        cg = c_ref[:, g * STATE:(g + 1) * STATE]

        def main(k, carry):
            t = g * tpg + k
            here = pl.ds(pl.multiple_of(t * tile, 128), tile)
            get = spread_of(t)
            put = gather_of(t)
            s_in = jnp.concatenate([sin[t * per + m, 0] for m in range(per)], 1)
            ds_in = jnp.concatenate([sin[t * per + m, 1] for m in range(per)], 1)
            x = x_ref[:, here].astype(F32)
            dy = dy_ref[:, here].astype(F32)
            dte = get(DT)
            ae = get(AA)
            xs = x * dte
            ady = (ae * dy).astype(BF)
            xt = xt_scr[:, here]
            y_in = get(GROW) * mm(cg, s_in)
            bds = mm(bg, ds_in)
            ys = []
            dxs = get(TAIL) * bds
            for i in range(nsub):
                r = SUB * (i + 1)
                lo = SUB * i
                be = get(B0 + i)
                bx = (be * xs[:r]).astype(BF)
                ad = ady[lo:r]
                ys.append(ae[lo:r] * mm(gm[g, lo:r, :r], bx))
                add = be * mm(gmt[g, i, :r], ad)
                if r < L:
                    add = jnp.concatenate([add, jnp.zeros((L - r, tile), F32)], 0)
                dxs = dxs + add
                dg[g, lo:r, :r] += mm(ad, bx, 1, 1)
            y = y_in + jnp.concatenate(ys, 0)
            dbc[0, g] += mm(xt, ds_in, 1, 1)
            dbc[1, g] += mm(dyg_scr[:, here], s_in, 1, 1)
            gx_ref[:, here] = (dxs * dte).astype(BF)
            end = jnp.sum(xt.astype(F32) * bds, 0, keepdims=True) + get(DEC)[:1] * jnp.sum(
                s_in.astype(F32) * ds_in.astype(F32), 0, keepdims=True)
            acc[0] += put(dxs * x)
            acc[1] += put(dy * y + jnp.where(is_last, end, 0.0))
            return carry

        lax.fori_loop(0, tpg, main, 0)
        dgm = jnp.where(causal, dg[g], 0.0).astype(BF)
        gcols = slice(g * STATE, (g + 1) * STATE)
        gc_ref[:, gcols] = dbc[1, g] + mm(dgm, bg)
        gb_ref[:, gcols] = dbc[0, g] + mm(dgm, cg, 0, 0)

    direct = acc[0]
    dcum = acc[1] - dt * direct
    dell = mm((ri <= ci).astype(F32), dcum, precision=high)
    gs_ref[...] = (direct - rate * dell) * (e / (1.0 + e))

    for d in range(1, nc):
        @pl.when(me + d < nc)
        def _():
            dkv_copy(d).wait_recv()
    summed = lax.fori_loop(
        1, nc - me, lambda d, s: s + dkvin[d].astype(F32), dkv[me].astype(F32)).astype(BF)
    for h in range(nh):
        kvb[0, h] = summed[h * rows:(h + 1) * rows, :kc]
        kvb[1, h] = summed[h * rows:(h + 1) * rows, kc:]
    for n, ref in enumerate((gk_ref, gv_ref)):
        for d in range(1, nh):
            peer = lax.rem(mh + d, nh)
            cp = remote(kvb.at[n, peer], cols(ref, mh, kc), back_send.at[1 + n, d],
                        back_recv.at[1 + n, d], "head", peer)
            cp.start()
            back.append(cp)
        ref[:, pl.ds(pl.multiple_of(mh * kc, 128), kc)] = kvb[n, mh]
    for cp in back:
        cp.wait_recv()
    for cp in head_copies + bk_copies + back:
        cp.wait_send()
    for d in range(1, nc):
        @pl.when(me + d < nc)
        def _():
            kv_copy(d).wait_send()

        @pl.when(me - d >= 0)
        def _():
            dkv_copy(d).wait_send()


def per_device(nc, nh, *args):
    x, step, decay, b, c, dy, q, k, v, o = args
    L, CH = x.shape
    H = step.shape[1]
    groups = b.shape[1] // STATE
    rows = q.shape[0]
    qc = q.shape[1] // nh
    kc = k.shape[1] // nh
    nkv = kc // HEAD_DIM
    chunk = CH // nc
    tile = min(512, CH // groups)
    nsub = L // SUB
    vrows = 4 * L + sum(SUB * (i + 1) for i in range(nsub)) + 16
    vm = pl.BlockSpec(memory_space=pltpu.VMEM)
    sem = pltpu.SemaphoreType.DMA
    V = pltpu.VMEM
    scratch = [
        V((nh, rows, qc), BF), V((nh, rows, qc), BF), V((nh, rows, kc), BF), V((nh, rows, kc), BF),
        V((nc, nh, rows, 2 * kc), BF), V((nc, L, 2 * kc), BF), V((nc, L, 2 * kc), BF),
        V((2, nh, rows, kc), BF),
        V((nkv, GROUP * L, HEAD_DIM), BF), V((nkv, GROUP * L, HEAD_DIM), BF),
        V((nh, rows, qc), BF),
        V((nc, L, GROUP * L), F32), V((nc, L, GROUP * L), F32),
        V((nc, 2, STATE, chunk), BF), V((nc, 2, STATE, chunk), BF), V((nc, 2, STATE, chunk), BF),
        V((nc, 8, chunk), F32), V((nc, 8, chunk), F32),
        V((vrows, H), BF), V((vrows, H), BF),
        V((L, CH), BF), V((L, CH), BF),
        V((groups, L, L), BF), V((groups, nsub, L, SUB), BF), V((groups, L, L), F32),
        V((2, L, H), F32), V((2, groups, L, STATE), F32),
        sem((4, nh)), sem((4, nh)), sem((nc,)), sem((nc,)), sem((nc,)), sem((nc,)),
        sem((nc,)), sem((nc,)), sem((nc,)), sem((nc,)), sem((nc,)), sem((nc,)),
        sem((3, nh)), sem((3, nh)),
    ]
    outs = (
        jax.ShapeDtypeStruct(x.shape, BF), jax.ShapeDtypeStruct(step.shape, F32),
        jax.ShapeDtypeStruct(b.shape, F32), jax.ShapeDtypeStruct(c.shape, F32),
        jax.ShapeDtypeStruct(q.shape, BF), jax.ShapeDtypeStruct(k.shape, BF),
        jax.ShapeDtypeStruct(v.shape, BF),
    )
    return pl.pallas_call(
        functools.partial(body, nc, nh, tile),
        out_shape=outs,
        in_specs=[vm] * 10,
        out_specs=[vm] * 7,
        scratch_shapes=scratch,
        compiler_params=pltpu.CompilerParams(
            collective_id=0, has_side_effects=True, vmem_limit_bytes=63 * 1024 * 1024),
    )(x, step, decay.reshape(1, H), b, c, dy, q, k, v, o)


def solution(mesh):
    nc, nh = mesh.shape["ctx"], mesh.shape["head"]
    tok = P(("ctx", "head"), None)
    both = P("ctx", "head")
    return jax.shard_map(
        functools.partial(per_device, nc, nh),
        mesh=mesh,
        in_specs=(both, both, P("head"), both, both, both, tok, tok, tok, tok),
        out_specs=(both, both, both, both, tok, tok, tok),
        check_vma=False,
    )
```

profile of v0, /device:TPU:0, one launch (start us, length us, event | category | flops | bytes accessed | tf_op | source)
XLA Modules:
  0.0 108.2 jit_solution(15043116251278550983)
XLA Ops:
  0.6 1.6 %copy.17.step_ref = f32[192,64]{1,0:T(8,128)} copy(f32[192,64]{0,1:T(8,128)} %param.11) | data formatting | bytes 98304 | tf_op args[1]
  2.2 98.2 %shard_map.153 = (bf16[192,4096]{1,0:T(8,128)(2,1)}, f32[192,64]{1,0:T(8,128)}, f32[192,256]{1,0:T(8,128)}, f32[192,256]{1,0:T(8,128)}, bf16[48,4096]{1,0:T(8,12...) custom-call(bf16[192,4096]{1,0:T(8,128)(2,1)} %x_ref.1, f32[192,64]{1,0:T(8,128)} %copy.17.step_ref, ...), custom_call_target="tpu_custom_call" | custom-call | tf_op jit(solution)/shard_map/pallas_call | solution.py:422
  100.5 1.6 %copy.18 = f32[192,64]{0,1:T(8,128)} copy(f32[192,64]{1,0:T(8,128)} %get-tuple-element.8) | data formatting | bytes 98304 | tf_op jit(solution)/shard_map/pallas_call | solution.py:422
  102.1 0.0 copy-start.2
  102.1 0.0 copy-start.1
  102.1 0.0 copy-start
  102.1 2.8 %copy.25 = bf16[192,4096]{1,0:T(8,128)(2,1)} copy(bf16[192,4096]{1,0:T(8,128)(2,1)} %get-tuple-element.21) | data formatting | bytes 3145728
  104.8 0.0 copy-done.2
  104.9 0.0 copy-start.4
  104.9 0.0 copy-start.3
  104.9 0.7 copy.26
  105.5 0.0 copy-done.1
  105.5 0.7 copy.27
  106.2 0.0 copy-done
  106.2 0.7 copy.28
  107.0 0.0 copy-done.4
  107.0 0.6 copy.29
  107.6 0.0 copy-done.3
  107.6 0.6 copy.30
Async XLA Ops:
  102.1 2.8 %copy-start.2 = (f32[192,256]{1,0:T(8,128)S(1)}, f32[192,256]{1,0:T(8,128)}, u32[]{:S(2)}) copy-start(f32[192,256]{1,0:T(8,128)} %get-tuple-element.23) | copy-start | bytes 589828
  102.1 3.5 %copy-start.1 = (f32[192,256]{1,0:T(8,128)S(1)}, f32[192,256]{1,0:T(8,128)}, u32[]{:S(2)}) copy-start(f32[192,256]{1,0:T(8,128)} %get-tuple-element.24) | copy-start | bytes 589828
  102.1 4.1 %copy-start = (bf16[48,4096]{1,0:T(8,128)(2,1)S(1)}, bf16[48,4096]{1,0:T(8,128)(2,1)}, u32[]{:S(2)}) copy-start(bf16[48,4096]{1,0:T(8,128)(2,1)} %get-tuple-element.25) | copy-start | bytes 1179652
  104.9 2.1 %copy-start.4 = (bf16[48,1024]{1,0:T(8,128)(2,1)S(1)}, bf16[48,1024]{1,0:T(8,128)(2,1)}, u32[]{:S(2)}) copy-start(bf16[48,1024]{1,0:T(8,128)(2,1)} %get-tuple-element.26) | copy-start | bytes 294916
  104.9 2.8 %copy-start.3 = (bf16[48,1024]{1,0:T(8,128)(2,1)S(1)}, bf16[48,1024]{1,0:T(8,128)(2,1)}, u32[]{:S(2)}) copy-start(bf16[48,1024]{1,0:T(8,128)(2,1)} %get-tuple-element.27) | copy-start | bytes 294916
where the time goes:
time: 110 us; the launch traced here: 108 us
  Pallas kernels  98.2 us (89%)
  local copies, waits for them, and re-layouts  9.36 us (9%)
    pallas_call x1, Pallas kernels, per_device(): pl.pallas_call(functools.partial(body, nc, nh, tile), out_shape=outs, in_...  98.2 us
    unnamed x17, local copies, waits for them, and re-layouts  7.75 us

commit v1 on v0

--- a/solution.py
+++ b/solution.py
@@ -35,12 +35,12 @@
     qbuf, obuf, kbuf, vbuf, kv, dkv, dkvin, kvb, q4, o4, dqb,
     s_scr, dp_scr,
     sloc, srecv, sin, decloc, decrecv,
-    vec_hi, vec_lo, xt_scr, dyg_scr, gm, gmt, dg, acc, dbc,
+    vec, xt_scr, dyg_scr, gm, gmt, dg, acc, dbc,
     h_send, h_recv, kv_send, kv_recv, st_send, st_recv, dc_send, dc_recv,
     bk_send, bk_recv, dkv_send, dkv_recv, back_send, back_recv,
 ):
     L, CH = x_ref.shape
-    H = step_ref.shape[1]
+    H = step_ref.shape[0]
     width = CH // H
     groups = b_ref.shape[1] // STATE
     rows = q_ref.shape[0]
@@ -72,19 +72,27 @@
     def cols(ref, at, n):
         return ref.at[:, pl.ds(pl.multiple_of(at * n, 128), n)]
 
+    qk = qc // nkv
+    moves = [(k_ref, kbuf, kc, 0, kc), (v_ref, vbuf, kc, 0, kc)]
+    for k in range(nkv):
+        moves += [(q_ref, qbuf.at[k], qc, k * qk, qk), (o_ref, obuf.at[k], qc, k * qk, qk)]
+
+    def part_of(at, w, off, n):
+        return pl.ds(pl.multiple_of(at * w + off, 128), n)
+
     head_copies = []
-    for n, (ref, buf, w) in enumerate(
-        ((k_ref, kbuf, kc), (v_ref, vbuf, kc), (q_ref, qbuf, qc), (o_ref, obuf, qc))):
+    for n, (ref, buf, w, off, size) in enumerate(moves):
         for d in range(1, nh):
             peer = lax.rem(mh + d, nh)
-            cp = remote(cols(ref, peer, w), buf.at[mh], h_send.at[n, d], h_recv.at[n, d], "head", peer)
+            cp = remote(ref.at[:, part_of(peer, w, off, size)], buf.at[mh],
+                        h_send.at[n, d], h_recv.at[n, d], "head", peer)
             cp.start()
             head_copies.append(cp)
-    for ref, buf, w in ((k_ref, kbuf, kc), (v_ref, vbuf, kc), (q_ref, qbuf, qc), (o_ref, obuf, qc)):
-        buf[mh] = ref[:, pl.ds(pl.multiple_of(mh * w, 128), w)]
+    for ref, buf, w, off, size in moves:
+        buf[mh] = ref[:, part_of(mh, w, off, size)]
 
     high = lax.Precision.HIGHEST
-    raw = step_ref[...]
+    raw = step_ref[...].T
     e = jnp.exp(raw)
     dt = jnp.log1p(e)
     rate = jnp.exp(decay_ref[...])
@@ -104,18 +112,18 @@
     for v in vecs:
         hi, lo = split(v)
         offs.append((at, v.shape[0]))
-        vec_hi[at:at + v.shape[0]] = hi
-        vec_lo[at:at + v.shape[0]] = lo
+        vec[at:at + v.shape[0], :H] = hi
+        vec[at:at + v.shape[0], H:] = lo
         at += v.shape[0]
 
     def spread_of(t):
-        hr = lax.broadcasted_iota(jnp.int32, (H, tile), 0)
-        hc = lax.broadcasted_iota(jnp.int32, (H, tile), 1)
+        hr = lax.rem(lax.broadcasted_iota(jnp.int32, (2 * H, tile), 0), H)
+        hc = lax.broadcasted_iota(jnp.int32, (2 * H, tile), 1)
         one = (hc // width + t * (tile // width) == hr).astype(F32).astype(BF)
 
         def get(n):
             o, r = offs[n]
-            return mm(vec_hi[o:o + r], one) + mm(vec_lo[o:o + r], one)
+            return mm(vec[o:o + r], one)
         return get
 
     def gather_of(t):
@@ -130,6 +138,20 @@
 
     DT, AA, GROW, TAIL, B0 = 0, 1, 2, 3, 4
     DEC = B0 + nsub
+
+    def kv_copy(d):
+        return remote(kv.at[me], kv.at[me], kv_send.at[d], kv_recv.at[d], "ctx", lax.rem(me + d, nc))
+
+    def send_kv():
+        for cp in head_copies[:2 * (nh - 1)]:
+            cp.wait_recv()
+        for h in range(nh):
+            kv[me, h, :, :kc] = kbuf[h]
+            kv[me, h, :, kc:] = vbuf[h]
+        for d in range(1, nc):
+            @pl.when(me + d < nc)
+            def _():
+                kv_copy(d).start()
 
     for g in range(groups):
         bg = b_ref[:, g * STATE:(g + 1) * STATE]
@@ -154,6 +176,8 @@
             return carry
 
         lax.fori_loop(0, tpg, summary, 0)
+        if g == 0:
+            send_kv()
 
     st_copies = []
     for d in range(1, nc):
@@ -166,50 +190,29 @@
     srecv[me] = sloc[me]
     decrecv[me] = decloc[me]
 
-    for cp in head_copies[:2 * (nh - 1)]:
-        cp.wait_recv()
-    for h in range(nh):
-        kv[me, h, :, :kc] = kbuf[h]
-        kv[me, h, :, kc:] = vbuf[h]
-
-    def kv_copy(d):
-        return remote(kv.at[me], kv.at[me], kv_send.at[d], kv_recv.at[d], "ctx", lax.rem(me + d, nc))
-
-    for d in range(1, nc):
-        @pl.when(me + d < nc)
-        def _():
-            kv_copy(d).start()
-
-    for cp in head_copies[2 * (nh - 1):]:
-        cp.wait_recv()
-    for src, dst in ((qbuf, q4), (obuf, o4)):
-        for k in range(nkv):
-            for i in range(GROUP):
-                for h in range(nh):
-                    c0 = (k * GROUP + i) * HEAD_DIM
-                    dst[k, i * L + h * rows:i * L + (h + 1) * rows] = src[h, :, c0:c0 + HEAD_DIM]
-
-    for cp in st_copies:
-        cp.wait()
-
-    def prefix(n, run):
-        sloc[n, 0] = run.astype(BF)
-        return decrecv[n][:1] * run + srecv[n, 0].astype(F32)
-
-    def suffix(n, run):
-        n = nc - 1 - n
-        sloc[n, 1] = run.astype(BF)
-        return decrecv[n][:1] * run + srecv[n, 1].astype(F32)
-
-    lax.fori_loop(0, nc, prefix, jnp.zeros((STATE, chunk), F32))
-    lax.fori_loop(0, nc, suffix, jnp.zeros((STATE, chunk), F32))
     bk_copies = []
-    for d in range(1, nc):
-        peer = lax.rem(me + d, nc)
-        cp = remote(sloc.at[peer], sin.at[me], bk_send.at[d], bk_recv.at[d], "ctx", peer)
-        cp.start()
-        bk_copies.append(cp)
-    sin[me] = sloc[me]
+
+    def pass_states():
+        for cp in st_copies:
+            cp.wait()
+
+        def prefix(n, run):
+            sloc[n, 0] = run.astype(BF)
+            return decrecv[n][:1] * run + srecv[n, 0].astype(F32)
+
+        def suffix(n, run):
+            n = nc - 1 - n
+            sloc[n, 1] = run.astype(BF)
+            return decrecv[n][:1] * run + srecv[n, 1].astype(F32)
+
+        lax.fori_loop(0, nc, prefix, jnp.zeros((STATE, chunk), F32))
+        lax.fori_loop(0, nc, suffix, jnp.zeros((STATE, chunk), F32))
+        for d in range(1, nc):
+            peer = lax.rem(me + d, nc)
+            cp = remote(sloc.at[peer], sin.at[me], bk_send.at[d], bk_recv.at[d], "ctx", peer)
+            cp.start()
+            bk_copies.append(cp)
+        sin[me] = sloc[me]
 
     for d in range(1, nc):
         @pl.when(me - d >= 0)
@@ -223,6 +226,14 @@
     diag4 = jnp.concatenate([diag] * GROUP, 1)
 
     for k in range(nkv):
+        for n in (2 + 2 * k, 3 + 2 * k):
+            for cp in head_copies[n * (nh - 1):(n + 1) * (nh - 1)]:
+                cp.wait_recv()
+        for src, dst in ((qbuf, q4), (obuf, o4)):
+            for i in range(GROUP):
+                for h in range(nh):
+                    dst[k, i * L + h * rows:i * L + (h + 1) * rows] = src[
+                        k, h, :, i * HEAD_DIM:(i + 1) * HEAD_DIM]
         kcol = slice(k * HEAD_DIM, (k + 1) * HEAD_DIM)
         vcol = slice(kc + k * HEAD_DIM, kc + (k + 1) * HEAD_DIM)
 
@@ -262,6 +273,8 @@
             for h in range(nh):
                 c0 = (k * GROUP + i) * HEAD_DIM
                 dqb[h, :, c0:c0 + HEAD_DIM] = dq[i * L + h * rows:i * L + (h + 1) * rows]
+        if k == 0:
+            pass_states()
 
     def dkv_copy(d):
         peer = lax.rem(me - d + nc, nc)
@@ -292,6 +305,25 @@
     dbc[...] = jnp.zeros_like(dbc)
     for cp in bk_copies:
         cp.wait_recv()
+
+    def home():
+        for d in range(1, nc):
+            @pl.when(me + d < nc)
+            def _():
+                dkv_copy(d).wait_recv()
+        summed = lax.fori_loop(
+            1, nc - me, lambda d, s: s + dkvin[d].astype(F32), dkv[me].astype(F32)).astype(BF)
+        for h in range(nh):
+            kvb[0, h] = summed[h * rows:(h + 1) * rows, :kc]
+            kvb[1, h] = summed[h * rows:(h + 1) * rows, kc:]
+        for n, ref in enumerate((gk_ref, gv_ref)):
+            for d in range(1, nh):
+                peer = lax.rem(mh + d, nh)
+                cp = remote(kvb.at[n, peer], cols(ref, mh, kc), back_send.at[1 + n, d],
+                            back_recv.at[1 + n, d], "head", peer)
+                cp.start()
+                back.append(cp)
+            ref[:, pl.ds(pl.multiple_of(mh * kc, 128), kc)] = kvb[n, mh]
 
     is_last = lax.broadcasted_iota(jnp.int32, (L, tile), 0) == L - 1
     for g in range(groups):
@@ -339,6 +371,8 @@
             return carry
 
         lax.fori_loop(0, tpg, main, 0)
+        if g == 0:
+            home()
         dgm = jnp.where(causal, dg[g], 0.0).astype(BF)
         gcols = slice(g * STATE, (g + 1) * STATE)
         gc_ref[:, gcols] = dbc[1, g] + mm(dgm, bg)
@@ -347,25 +381,8 @@
     direct = acc[0]
     dcum = acc[1] - dt * direct
     dell = mm((ri <= ci).astype(F32), dcum, precision=high)
-    gs_ref[...] = (direct - rate * dell) * (e / (1.0 + e))
-
-    for d in range(1, nc):
-        @pl.when(me + d < nc)
-        def _():
-            dkv_copy(d).wait_recv()
-    summed = lax.fori_loop(
-        1, nc - me, lambda d, s: s + dkvin[d].astype(F32), dkv[me].astype(F32)).astype(BF)
-    for h in range(nh):
-        kvb[0, h] = summed[h * rows:(h + 1) * rows, :kc]
-        kvb[1, h] = summed[h * rows:(h + 1) * rows, kc:]
-    for n, ref in enumerate((gk_ref, gv_ref)):
-        for d in range(1, nh):
-            peer = lax.rem(mh + d, nh)
-            cp = remote(kvb.at[n, peer], cols(ref, mh, kc), back_send.at[1 + n, d],
-                        back_recv.at[1 + n, d], "head", peer)
-            cp.start()
-            back.append(cp)
-        ref[:, pl.ds(pl.multiple_of(mh * kc, 128), kc)] = kvb[n, mh]
+    gs_ref[...] = ((direct - rate * dell) * (e / (1.0 + e))).T
+
     for cp in back:
         cp.wait_recv()
     for cp in head_copies + bk_copies + back:
@@ -397,7 +414,7 @@
     sem = pltpu.SemaphoreType.DMA
     V = pltpu.VMEM
     scratch = [
-        V((nh, rows, qc), BF), V((nh, rows, qc), BF), V((nh, rows, kc), BF), V((nh, rows, kc), BF),
+        V((nkv, nh, rows, qc // nkv), BF), V((nkv, nh, rows, qc // nkv), BF), V((nh, rows, kc), BF), V((nh, rows, kc), BF),
         V((nc, nh, rows, 2 * kc), BF), V((nc, L, 2 * kc), BF), V((nc, L, 2 * kc), BF),
         V((2, nh, rows, kc), BF),
         V((nkv, GROUP * L, HEAD_DIM), BF), V((nkv, GROUP * L, HEAD_DIM), BF),
@@ -405,21 +422,21 @@
         V((nc, L, GROUP * L), F32), V((nc, L, GROUP * L), F32),
         V((nc, 2, STATE, chunk), BF), V((nc, 2, STATE, chunk), BF), V((nc, 2, STATE, chunk), BF),
         V((nc, 8, chunk), F32), V((nc, 8, chunk), F32),
-        V((vrows, H), BF), V((vrows, H), BF),
+        V((vrows, 2 * H), BF),
         V((L, CH), BF), V((L, CH), BF),
         V((groups, L, L), BF), V((groups, nsub, L, SUB), BF), V((groups, L, L), F32),
         V((2, L, H), F32), V((2, groups, L, STATE), F32),
-        sem((4, nh)), sem((4, nh)), sem((nc,)), sem((nc,)), sem((nc,)), sem((nc,)),
+        sem((2 + 2 * nkv, nh)), sem((2 + 2 * nkv, nh)), sem((nc,)), sem((nc,)), sem((nc,)), sem((nc,)),
         sem((nc,)), sem((nc,)), sem((nc,)), sem((nc,)), sem((nc,)), sem((nc,)),
         sem((3, nh)), sem((3, nh)),
     ]
     outs = (
-        jax.ShapeDtypeStruct(x.shape, BF), jax.ShapeDtypeStruct(step.shape, F32),
+        jax.ShapeDtypeStruct(x.shape, BF), jax.ShapeDtypeStruct((H, L), F32),
         jax.ShapeDtypeStruct(b.shape, F32), jax.ShapeDtypeStruct(c.shape, F32),
         jax.ShapeDtypeStruct(q.shape, BF), jax.ShapeDtypeStruct(k.shape, BF),
         jax.ShapeDtypeStruct(v.shape, BF),
     )
-    return pl.pallas_call(
+    res = pl.pallas_call(
         functools.partial(body, nc, nh, tile),
         out_shape=outs,
         in_specs=[vm] * 10,
@@ -427,7 +444,8 @@
         scratch_shapes=scratch,
         compiler_params=pltpu.CompilerParams(
             collective_id=0, has_side_effects=True, vmem_limit_bytes=63 * 1024 * 1024),
-    )(x, step, decay.reshape(1, H), b, c, dy, q, k, v, o)
+    )(x, step.T, decay.reshape(1, H), b, c, dy, q, k, v, o)
+    return (res[0], res[1].T) + tuple(res[2:])
 
 
 def solution(mesh):

time: 110 us -> 114 us (1.036); the launches traced: 108 us -> 114 us
  Pallas kernels: 98.2 us -> 106 us
  local copies, waits for them, and re-layouts: 9.36 us -> 6.81 us
    pallas_call x1, Pallas kernels: 98.2 us -> 106 us  [per_device(): pl.pallas_call(functools.partial(body, nc, nh, tile), out_shape=outs, in_...]
    pallas_call x1 -> x0, local copies, waits for them, and re-layouts: 1.61 us -> none  [per_device(): pl.pallas_call(functools.partial(body, nc, nh, tile), out_shape=outs, in_...]
    unnamed x17 -> x19, local copies, waits for them, and re-layouts: 7.75 us -> 6.81 us
where the time goes in v1:
time: 114 us
  Pallas kernels  106 us (93%)
  local copies, waits for them, and re-layouts  6.81 us (6%)
    pallas_call x1, Pallas kernels, per_device(): pl.pallas_call(functools.partial(body, nc, nh, tile), out_shape=outs, in_...  106 us
    unnamed x19, local copies, waits for them, and re-layouts  6.81 us

profile of v1, /device:TPU:0, one launch (start us, length us, event | category | flops | bytes accessed | tf_op | source)
XLA Modules:
  0.0 113.7 jit_solution(3585820961528302176)
XLA Ops:
  0.6 106.2 %shard_map.153 = (bf16[192,4096]{1,0:T(8,128)(2,1)}, f32[64,192]{1,0:T(8,128)}, f32[192,256]{1,0:T(8,128)}, f32[192,256]{1,0:T(8,128)}, bf16[48,4096]{1,0:T(8,12...) custom-call(bf16[192,4096]{1,0:T(8,128)(2,1)} %x_ref.1, f32[64,192]{1,0:T(8,128)} %bitcast.3, ...), custom_call_target="tpu_custom_call" | custom-call | tf_op jit(solution)/shard_map/pallas_call | solution.py:439
  106.9 0.0 copy-start.5
  106.9 0.0 copy-start.2
  106.9 0.0 copy-start.1
  106.9 0.0 copy-start
  106.9 2.8 %copy.24 = bf16[192,4096]{1,0:T(8,128)(2,1)} copy(bf16[192,4096]{1,0:T(8,128)(2,1)} %get-tuple-element.28) | data formatting | bytes 3145728
  109.7 0.0 copy-done.5
  109.7 0.0 copy-start.4
  109.7 0.0 copy-start.3
  109.7 0.6 copy.25
  110.3 0.0 copy-done.2
  110.3 0.7 copy.26
  111.0 0.0 copy-done.1
  111.0 0.7 copy.27
  111.7 0.0 copy-done
  111.7 0.7 copy.28
  112.4 0.0 copy-done.4
  112.4 0.6 copy.29
  113.1 0.0 copy-done.3
  113.1 0.6 copy.30
Async XLA Ops:
  106.9 2.8 %copy-start.5 = (f32[64,192]{1,0:T(8,128)S(1)}, f32[64,192]{1,0:T(8,128)}, u32[]{:S(2)}) copy-start(f32[64,192]{1,0:T(8,128)} %get-tuple-element.15) | copy-start | bytes 147460
  106.9 3.4 %copy-start.2 = (f32[192,256]{1,0:T(8,128)S(1)}, f32[192,256]{1,0:T(8,128)}, u32[]{:S(2)}) copy-start(f32[192,256]{1,0:T(8,128)} %get-tuple-element.30) | copy-start | bytes 589828
  106.9 4.1 %copy-start.1 = (f32[192,256]{1,0:T(8,128)S(1)}, f32[192,256]{1,0:T(8,128)}, u32[]{:S(2)}) copy-start(f32[192,256]{1,0:T(8,128)} %get-tuple-element.31) | copy-start | bytes 589828
  106.9 4.8 %copy-start = (bf16[48,4096]{1,0:T(8,128)(2,1)S(1)}, bf16[48,4096]{1,0:T(8,128)(2,1)}, u32[]{:S(2)}) copy-start(bf16[48,4096]{1,0:T(8,128)(2,1)} %get-tuple-element.32) | copy-start | bytes 1179652
  109.7 2.7 %copy-start.4 = (bf16[48,1024]{1,0:T(8,128)(2,1)S(1)}, bf16[48,1024]{1,0:T(8,128)(2,1)}, u32[]{:S(2)}) copy-start(bf16[48,1024]{1,0:T(8,128)(2,1)} %get-tuple-element.33) | copy-start | bytes 294916
  109.7 3.4 %copy-start.3 = (bf16[48,1024]{1,0:T(8,128)(2,1)S(1)}, bf16[48,1024]{1,0:T(8,128)(2,1)}, u32[]{:S(2)}) copy-start(bf16[48,1024]{1,0:T(8,128)(2,1)} %get-tuple-element.34) | copy-start | bytes 294916

commit v2 on v1

--- a/solution.py
+++ b/solution.py
@@ -176,8 +176,6 @@
             return carry
 
         lax.fori_loop(0, tpg, summary, 0)
-        if g == 0:
-            send_kv()
 
     st_copies = []
     for d in range(1, nc):
@@ -189,6 +187,7 @@
             st_copies.append(cp)
     srecv[me] = sloc[me]
     decrecv[me] = decloc[me]
+    send_kv()
 
     bk_copies = []
 
@@ -213,6 +212,8 @@
             cp.start()
             bk_copies.append(cp)
         sin[me] = sloc[me]
+
+    pass_states()
 
     for d in range(1, nc):
         @pl.when(me - d >= 0)
@@ -273,8 +274,6 @@
             for h in range(nh):
                 c0 = (k * GROUP + i) * HEAD_DIM
                 dqb[h, :, c0:c0 + HEAD_DIM] = dq[i * L + h * rows:i * L + (h + 1) * rows]
-        if k == 0:
-            pass_states()
 
     def dkv_copy(d):
         peer = lax.rem(me - d + nc, nc)
@@ -371,8 +370,6 @@
             return carry
 
         lax.fori_loop(0, tpg, main, 0)
-        if g == 0:
-            home()
         dgm = jnp.where(causal, dg[g], 0.0).astype(BF)
         gcols = slice(g * STATE, (g + 1) * STATE)
         gc_ref[:, gcols] = dbc[1, g] + mm(dgm, bg)
@@ -383,6 +380,7 @@
     dell = mm((ri <= ci).astype(F32), dcum, precision=high)
     gs_ref[...] = ((direct - rate * dell) * (e / (1.0 + e))).T
 
+    home()
     for cp in back:
         cp.wait_recv()
     for cp in head_copies + bk_copies + back:

time: 114 us -> 105 us (0.921)
  Pallas kernels: 106 us -> 97.5 us
    pallas_call x1, Pallas kernels: 106 us -> 97.5 us  [per_device(): pl.pallas_call(functools.partial(body, nc, nh, tile), out_shape=outs, in_...]
where the time goes in v2:
time: 105 us
  Pallas kernels  97.5 us (93%)
  local copies, waits for them, and re-layouts  6.81 us (6%)
    pallas_call x1, Pallas kernels, per_device(): pl.pallas_call(functools.partial(body, nc, nh, tile), out_shape=outs, in_...  97.5 us
    unnamed x19, local copies, waits for them, and re-layouts  6.81 us

profile of v2, /device:TPU:0, one launch (start us, length us, event | category | flops | bytes accessed | tf_op | source)
XLA Modules:
  0.0 105.0 jit_solution(1975857770188498736)
XLA Ops:
  0.6 97.5 %shard_map.153 = (bf16[192,4096]{1,0:T(8,128)(2,1)}, f32[64,192]{1,0:T(8,128)}, f32[192,256]{1,0:T(8,128)}, f32[192,256]{1,0:T(8,128)}, bf16[48,4096]{1,0:T(8,12...) custom-call(bf16[192,4096]{1,0:T(8,128)(2,1)} %x_ref.1, f32[64,192]{1,0:T(8,128)} %bitcast.3, ...), custom_call_target="tpu_custom_call" | custom-call | tf_op jit(solution)/shard_map/pallas_call | solution.py:437
  98.2 0.0 copy-start.5
  98.2 0.0 copy-start.2
  98.2 0.0 copy-start.1
  98.2 0.0 copy-start
  98.2 2.8 %copy.24 = bf16[192,4096]{1,0:T(8,128)(2,1)} copy(bf16[192,4096]{1,0:T(8,128)(2,1)} %get-tuple-element.28) | data formatting | bytes 3145728
  101.0 0.0 copy-done.5
  101.0 0.0 copy-start.4
  101.0 0.0 copy-start.3
  101.0 0.6 copy.25
  101.6 0.0 copy-done.2
  101.6 0.7 copy.26
  102.3 0.0 copy-done.1
  102.3 0.7 copy.27
  103.0 0.0 copy-done
  103.0 0.7 copy.28
  103.7 0.0 copy-done.4
  103.7 0.6 copy.29
  104.4 0.0 copy-done.3
  104.4 0.6 copy.30
Async XLA Ops:
  98.2 2.8 %copy-start.5 = (f32[64,192]{1,0:T(8,128)S(1)}, f32[64,192]{1,0:T(8,128)}, u32[]{:S(2)}) copy-start(f32[64,192]{1,0:T(8,128)} %get-tuple-element.15) | copy-start | bytes 147460
  98.2 3.4 %copy-start.2 = (f32[192,256]{1,0:T(8,128)S(1)}, f32[192,256]{1,0:T(8,128)}, u32[]{:S(2)}) copy-start(f32[192,256]{1,0:T(8,128)} %get-tuple-element.30) | copy-start | bytes 589828
  98.2 4.1 %copy-start.1 = (f32[192,256]{1,0:T(8,128)S(1)}, f32[192,256]{1,0:T(8,128)}, u32[]{:S(2)}) copy-start(f32[192,256]{1,0:T(8,128)} %get-tuple-element.31) | copy-start | bytes 589828
  98.2 4.8 %copy-start = (bf16[48,4096]{1,0:T(8,128)(2,1)S(1)}, bf16[48,4096]{1,0:T(8,128)(2,1)}, u32[]{:S(2)}) copy-start(bf16[48,4096]{1,0:T(8,128)(2,1)} %get-tuple-element.32) | copy-start | bytes 1179652
  101.0 2.7 %copy-start.4 = (bf16[48,1024]{1,0:T(8,128)(2,1)S(1)}, bf16[48,1024]{1,0:T(8,128)(2,1)}, u32[]{:S(2)}) copy-start(bf16[48,1024]{1,0:T(8,128)(2,1)} %get-tuple-element.33) | copy-start | bytes 294916
  101.0 3.4 %copy-start.3 = (bf16[48,1024]{1,0:T(8,128)(2,1)S(1)}, bf16[48,1024]{1,0:T(8,128)(2,1)}, u32[]{:S(2)}) copy-start(bf16[48,1024]{1,0:T(8,128)(2,1)} %get-tuple-element.34) | copy-start | bytes 294916
